TPU v7x, 256 devices: a whole 4x4x8 slice. The times are simulated.
256 devices in a mesh: own: 8 (over z), col: 8 (over x, core), mlp: 4 (over y).
Axes of the slice: x: 4, y: 4, z: 8, core: 2. Of those that a mesh axis runs over, the one named last changes fastest.
Arguments:
- features: bfloat16 [262144, 512], P(('own', 'col')), may hold values from -6 to 6
- nbr_page: int32 [8192, 32], P(('own', 'col')), may hold values from 0 to 262143, as said below
- nbr_weight: bfloat16 [8192, 32], P(('own', 'col')), may hold values from 0.0049743652 to 0.29882812
- labels: int32 [8192], P(('own', 'col')), may hold values from 0 to 255
- w_one: bfloat16 [512, 2048], P(None, 'mlp'), may hold values from -0.25 to 0.25
- w_two: bfloat16 [2048, 256], P('mlp'), may hold values from -0.125 to 0.125
Outputs:
- grad_one: float32 [512, 2048], P(None, 'mlp')
- grad_two: float32 [2048, 256], P('mlp')
Inputs may be any that keep to these rules, and one draw needn't show every extreme that they name: `nbr_page`: page p is held by owner p // 4096 (owners numbered along own then col) at its row p % 4096. The 32 neighbours of a target are distinct pages listed in non-decreasing order of owner. Of the 4096 neighbour entries of the targets of one index of own and col, at most 128 fall on one owner; one owner receives exactly 128 entries from every index, and some owners receive none from some indices.
All inputs are finite; a program needn't handle non-finite values.
Results may differ from a plain program's by a relative error of at most 0.011.
Values may be sent and summed in bfloat16 or wider, within the bound.
No kernel may reach another device: no remote copies, remote signals or barrier semaphores. Data moves between devices by JAX's collectives and lax.ppermute only.
A program may use at most 128 MiB of HBM per device.

v0:
```python
import jax
import jax.numpy as jnp
from jax import lax
from jax.sharding import PartitionSpec as P


def body(features, nbr_page, nbr_weight, labels, w_one, w_two):
    rows_dev = features.shape[0]
    width_f = features.shape[1]
    targets = nbr_page.shape[0]
    width_k = nbr_page.shape[1]
    owners = lax.axis_size(("own", "col"))
    entries = targets * width_k
    capacity = 2 * entries // owners
    owner_ids = nbr_page // rows_dev
    local_row = nbr_page % rows_dev
    owner_range = jnp.arange(owners, dtype=jnp.int32)
    matches = (owner_ids[:, :, None] == owner_range[None, None, :]).astype(jnp.int32)
    row_count = jnp.sum(matches, axis=1)
    earlier_rows = jnp.cumsum(row_count, axis=0) - row_count
    before_owner = jnp.cumsum(row_count, axis=1) - row_count
    first_slot = earlier_rows - before_owner + owner_range[None, :] * capacity
    slot_ids = (
        jnp.sum(matches * first_slot[:, None, :], axis=2)
        + jnp.arange(width_k, dtype=jnp.int32)[None, :]
    )
    flat_slot = slot_ids.reshape(-1)
    requests = jnp.zeros((owners * capacity,), jnp.int32).at[flat_slot].set(local_row.reshape(-1))
    requests = requests.reshape(owners, capacity)
    asked_rows = lax.all_to_all(requests, ("own", "col"), split_axis=0, concat_axis=0, tiled=True)
    fetched = features[asked_rows]
    returned = lax.all_to_all(fetched, ("own", "col"), split_axis=0, concat_axis=0, tiled=True)
    received = returned.reshape(owners * capacity, width_f)
    contract_first = (((0,), (0,)), ((), ()))
    target_ids = jnp.broadcast_to(
        jnp.arange(targets, dtype=jnp.int32)[:, None], (targets, width_k)
    ).reshape(-1)
    spread = (
        jnp.zeros((targets, owners * capacity), jnp.bfloat16)
        .at[target_ids, flat_slot]
        .set(nbr_weight.reshape(-1))
    )
    pre_act = jnp.dot(received, w_one, preferred_element_type=jnp.float32)
    active = jnp.maximum(pre_act, 0.0).astype(jnp.bfloat16)
    hidden = jnp.dot(spread, active, preferred_element_type=jnp.float32).astype(jnp.bfloat16)
    partial_logits = jnp.dot(hidden, w_two, preferred_element_type=jnp.float32)
    logits = lax.psum(partial_logits, "mlp")
    exponent = jnp.exp(logits)
    probability = exponent / jnp.sum(exponent, axis=1, keepdims=True)
    classes = w_two.shape[1]
    onehot_label = (labels[:, None] == jnp.arange(classes, dtype=jnp.int32)[None, :]).astype(
        jnp.float32
    )
    d_logits = (probability - onehot_label).astype(jnp.bfloat16)
    grad_two = lax.dot_general(hidden, d_logits, contract_first, preferred_element_type=jnp.float32)
    d_hidden = lax.dot_general(
        d_logits, w_two, (((1,), (1,)), ((), ())), preferred_element_type=jnp.float32
    ).astype(jnp.bfloat16)
    positive = (pre_act > 0).astype(jnp.float32)
    scattered = lax.dot_general(
        spread, d_hidden, contract_first, preferred_element_type=jnp.float32
    )
    d_pre = (scattered * positive).astype(jnp.bfloat16)
    grad_one = lax.dot_general(received, d_pre, contract_first, preferred_element_type=jnp.float32)
    grad_one, grad_two = lax.psum((grad_one, grad_two), ("own", "col"))
    return (grad_one, grad_two)


def solution(mesh):
    placed = (
        P(("own", "col"), None),
        P(("own", "col"), None),
        P(("own", "col"), None),
        P(("own", "col")),
        P(None, "mlp"),
        P("mlp", None),
    )
    return jax.shard_map(
        body,
        mesh=mesh,
        in_specs=placed,
        out_specs=(P(None, "mlp"), P("mlp", None)),
        check_vma=False,
    )
```

profile of v0, /device:TPU:8, one launch (start us, length us, event | category | flops | bytes accessed | tf_op | source)
XLA Modules:
  0.0 551.1 jit_solution(711926448814235918)
XLA Ops:
  7.2 0.0 copy-start
  7.2 0.8 add_select_fusion
  8.0 0.1 convert_reduce_fusion
  8.1 0.1 copy.16
  8.2 0.1 reduce_window_sum.23
  8.3 0.1 copy.18
  8.4 0.1 copy.22
  8.5 0.1 reshape.163
  8.6 0.2 reduce_window_sum.22
  8.8 0.1 copy.20
  8.8 0.2 select_reduce_fusion
  9.1 0.1 copy.21
  9.2 0.1 add.85
  9.3 0.1 reshape.145
  9.4 15.5 %scatter_custom_fusion = s32[8192]{0:T(1024)S(1)} fusion(s32[4096]{0:T(1024)S(1)} %bitcast.22, s32[4096]{0:T(1024)S(1)} %reshape.163, s32[]{:T(128)} %constant.41.clone.1), kind=kCustom, calls=%fused_computation.34 | custom fusion | bytes 32772 | tf_op jit(solution)/shard_map/scatter | solution.py:28
  25.0 21.3 %all_to_all.17 = s32[64,1,128]{2,1,0:T(1,128)S(1)} all-to-all(s32[64,1,128]{2,1,0:T(1,128)S(1)} %bitcast.23), channel_id=1, replica_groups=mesh['own'=8,'col'=8,'mlp'=4] {'own','col'}, dimensions={0} | all-to-all | bytes 65536 | tf_op jit(solution)/shard_map/all_to_all | solution.py:30
  46.3 36.5 %gather_fusion = bf16[8192,512]{1,0:T(8,128)(2,1)} fusion(bf16[4096,512]{1,0:T(8,128)(2,1)} %param.6, s32[8192]{0:T(1024)S(1)} %fusion.7), kind=kCustom, calls=%fused_computation | custom fusion | bytes 16809984 | tf_op jit(solution)/shard_map/gather | solution.py:31
  82.8 5.9 %all-to-all-start.1 = ((bf16[64,128,512]{2,1,0:T(8,128)(2,1)}), bf16[64,128,512]{2,1,0:T(8,128)(2,1)}, u32[]{:S(2)}, u32[]{:S(2)}) async-start(bf16[64,128,512]{2,1,0:T(8,128)(2,1)} %bitcast.21), calls=%async_computation.1 | async-start | bytes 16777216 | tf_op jit(solution)/shard_map/all_to_all | solution.py:32
  88.7 0.0 all-reduce.4.cloned.1.call-start
  88.8 0.0 copy-done.4
  88.8 0.1 copy.23
  88.9 0.1 reshape.169
  89.0 0.0 copy-done.7
  89.0 0.1 multiply_reduce_fusion
  89.1 0.0 copy-done.6
  89.1 0.1 and_reduce_fusion
  89.3 30.4 %scatter_custom_fusion.1 = bf16[1048576]{0:T(1024)(128)(2,1)} fusion(s32[4096]{0:T(1024)S(1)} %broadcast_select_fusion, bf16[4096]{0:T(1024)(128)(2,1)S(1)} %reshape.169, bf16[]{:T(256)} %constant.50.clone.1), kind=kCustom, calls=%fused_computation.10 | custom fusion | bytes 2097154
  119.7 2.8 reshape.150
  122.5 152.3 %all-to-all-done.1 = bf16[64,128,512]{2,1,0:T(8,128)(2,1)} async-done(((bf16[64,128,512]{2,1,0:T(8,128)(2,1)}), bf16[64,128,512]{2,1,0:T(8,128)(2,1)}, u32[]{:S(2)}, u32[]{:S(2)}) %all-to-all-start.1) | async-done | bytes 8388640 | tf_op jit(solution)/shard_map/all_to_all | solution.py:32
  274.8 0.0 copy-done
  274.8 7.1 %fusion.15 = f32[8192,512]{1,0:T(8,128)S(1)} fusion(bf16[8192,512]{1,0:T(8,128)(2,1)} %bitcast.5, bf16[512,512]{1,0:T(8,128)(2,1)S(1)} %copy-done), kind=kOutput, calls=%fused_computation.43 | convolution fusion | flops 4294967296 | bytes 25690112 | tf_op jit(solution)/shard_map/dot_general | solution.py:43
  281.9 0.0 copy-start.3
  281.9 0.0 copy-start.5
  281.9 1.6 fusion.3
  283.5 4.1 copy-done.1
  287.6 0.8 fusion.16
  288.4 0.0 all-reduce.4.cloned.1.call-update
  288.5 0.0 all-reduce.6.cloned.1.call-start
  288.5 42.6 %all-reduce.4.cloned.1.call-done = f32[128,256]{1,0:T(8,128)} async-done(((f32[128,256]{1,0:T(8,128)}), f32[128,256]{1,0:T(8,128)}) %all-reduce.4.cloned.1.call-update) | async-done | bytes 131088 | tf_op jit(solution)/shard_map/psum | solution.py:47
  331.1 1.0 exponential_reduce_fusion
  332.1 0.0 copy-done.5
  332.1 1.1 convolution_convert_fusion
  333.2 16.1 %fusion.2 = f32[512,512]{1,0:T(8,128)} fusion(bf16[8192,512]{1,0:T(8,128)(2,1)} %bitcast.5, f32[8192,512]{1,0:T(8,128)} %copy-done.1, bf16[128,8192]{1,0:T(8,128)(2,1)S(1)} %reshape.150, bf16[128,512]{1,0:T(8,128)(2,1)S(1)} %convolution_convert_fusion), kind=kOutput, calls=%fused_computation.7 | convolution fusion | flops 5381292032 | bytes 28442624 | tf_op jit(solution)/shard_map/dot_general | solution.py:64
  349.3 1.1 fusion.14
  350.4 0.0 all-reduce.6.cloned.1.call-update
  350.5 189.7 %all-reduce.6.cloned.1.call-done = (f32[512,512]{1,0:T(8,128)}, f32[512,256]{1,0:T(8,128)}) async-done(((f32[512,512]{1,0:T(8,128)}, f32[512,256]{1,0:T(8,128)}), (f32[512,512]{1,0:T(8,128)}, f32[512,256]{1,0:T(8,128)})) %all-reduce.6.cloned.1.call-update) | async-done | bytes 1572880 | tf_op jit(solution)/shard_map/psum | solution.py:65
  540.2 2.3 copy.27
  542.4 1.9 copy.28
  (14 shorter events, 0.1 us)
Async XLA Ops:
  7.2 267.6 %copy-start = (bf16[512,512]{1,0:T(8,128)(2,1)S(1)}, bf16[512,512]{1,0:T(8,128)(2,1)}, u32[]{:S(2)}) copy-start(bf16[512,512]{1,0:T(8,128)(2,1)} %param.10) | copy-start | bytes 1572868
  82.8 6.0 %copy-start.4 = (bf16[128,32]{0,1:T(8,128)(2,1)S(1)}, bf16[128,32]{0,1:T(8,128)(2,1)}, u32[]{:S(2)}) copy-start(bf16[128,32]{0,1:T(8,128)(2,1)} %param.8) | copy-start | bytes 24580
  82.8 6.2 %copy-start.7 = (s32[2]{0:T(128)S(1)}, s32[2]{0:T(128)}, u32[]{:S(2)}) copy-start(s32[2]{0:T(128)} %constant.51) | copy-start | bytes 28
  82.8 6.3 %copy-start.6 = (s32[2]{0:T(128)S(1)}, s32[2]{0:T(128)}, u32[]{:S(2)}) copy-start(s32[2]{0:T(128)} %constant.54) | copy-start | bytes 28
  82.8 191.9 %all-to-all-start.1 = ((bf16[64,128,512]{2,1,0:T(8,128)(2,1)}), bf16[64,128,512]{2,1,0:T(8,128)(2,1)}, u32[]{:S(2)}, u32[]{:S(2)}) async-start(bf16[64,128,512]{2,1,0:T(8,128)(2,1)} %bitcast.21), calls=%async_computation.1 | async-start | bytes 16777216 | tf_op jit(solution)/shard_map/all_to_all | solution.py:32
  88.7 242.3 %all-reduce.4.cloned.1.call-start = ((), (), s32[]{:S(2)}) async-start(), calls=%async_computation.2 | async-start | bytes 262144 | tf_op jit(solution)/shard_map/psum | solution.py:47
  281.9 5.7 %copy-start.1 = (f32[8192,512]{1,0:T(8,128)}, f32[8192,512]{1,0:T(8,128)S(1)}, u32[]{:S(2)}) copy-start(f32[8192,512]{1,0:T(8,128)S(1)} %fusion.15) | copy-start | bytes 50331652
  281.9 5.7 %copy-start.3 = (bf16[512,256]{1,0:T(8,128)(2,1)S(1)}, bf16[512,256]{1,0:T(8,128)(2,1)}, u32[]{:S(2)}) copy-start(bf16[512,256]{1,0:T(8,128)(2,1)} %param.11) | copy-start | bytes 786436
  281.9 50.2 %copy-start.5 = (s32[128]{0:T(128)S(1)}, s32[128]{0:T(128)}, u32[]{:S(2)}) copy-start(s32[128]{0:T(128)} %param.9) | copy-start | bytes 1540
  288.5 251.7 %all-reduce.6.cloned.1.call-start = ((), (), s32[]{:S(2)}) async-start(), calls=%async_computation.3 | async-start | bytes 3145728 | tf_op jit(solution)/shard_map/psum | solution.py:65
  333.2 16.1 %copy-start.2 = (f32[128,256]{1,0:T(8,128)S(1)}, f32[128,256]{1,0:T(8,128)}, u32[]{:S(2)}) copy-start(f32[128,256]{1,0:T(8,128)} %all-reduce.4.cloned.1.call-done) | copy-start | bytes 393220
Sparse Core Ops, SparseCore 0:
  288.6 42.4 all-reduce.3
  350.6 189.5 all-reduce.5
where the time goes:
time: 552 us; the launch traced here: 551 us
  waiting for transfers between devices  385 us (70%)
  local copies, waits for them, and re-layouts  94.5 us (17%)
  matrix products  27.8 us (5%)
  blocking collectives  21.3 us (4%)
  between operations  14.3 us (3%)
  starting transfers between devices  5.97 us (1%)
    psum x1, waiting for transfers between devices, body(): grad_one, grad_two = lax.psum((grad_one, grad_two), ('own', 'col'))  190 us
    all_to_all x1, waiting for transfers between devices, body(): lax.all_to_all(fetched, ('own', 'col'), split_axis=0, concat_axis=0, tile...  152 us
    psum x1, waiting for transfers between devices, body(): logits = lax.psum(partial_logits, 'mlp')  42.6 us
    unnamed x20, local copies, waits for them, and re-layouts  38.8 us
    gather x1, local copies, waits for them, and re-layouts, body(): fetched = features[asked_rows]  36.5 us
    all_to_all x1, blocking collectives, body(): lax.all_to_all(requests, ('own', 'col'), split_axis=0, concat_axis=0, til...  21.3 us
    dot_general x1, matrix products, body(): lax.dot_general(received, d_pre, contract_first, preferred_element_type=j...  16.1 us
    scatter x1, local copies, waits for them, and re-layouts, body(): jnp.zeros((owners * capacity,), jnp.int32).at[flat_slot]  15.5 us
  transfers between devices with their start and end apart: 3, of which 3 were waited for; matrix products, arithmetic and copies ran while one was open for 6% of the time, Pallas kernels for 0%

commit v1 on v0

--- a/solution.py
+++ b/solution.py
@@ -2,6 +2,12 @@
 import jax.numpy as jnp
 from jax import lax
 from jax.sharding import PartitionSpec as P
+
+
+def extend_area(local_array, group_axis, axis_tag):
+    for no in (group_axis, axis_tag):
+        local_array = lax.psum(local_array, no)
+    return local_array
 
 
 def body(features, nbr_page, nbr_weight, labels, w_one, w_two):
@@ -62,7 +68,7 @@
     )
     d_pre = (scattered * positive).astype(jnp.bfloat16)
     grad_one = lax.dot_general(received, d_pre, contract_first, preferred_element_type=jnp.float32)
-    grad_one, grad_two = lax.psum((grad_one, grad_two), ("own", "col"))
+    grad_one, grad_two = extend_area((grad_one, grad_two), "own", "col")
     return (grad_one, grad_two)
 
 

time: 552 us -> 513 us (0.929)
  waiting for transfers between devices: 385 us -> 347 us
    psum x1 -> x2, waiting for transfers between devices: 190 us -> 152 us  [extend_area(): local_array = lax.psum(local_array, no)]
  transfers between devices with their start and end apart: 3 -> 4, of which waited for: 3 -> 4; matrix products, arithmetic and copies ran while one was open for 6% -> 7% of each run, Pallas kernels for 0% -> 0%
where the time goes in v1:
time: 513 us
  waiting for transfers between devices  347 us (68%)
  local copies, waits for them, and re-layouts  94.5 us (18%)
  matrix products  27.8 us (5%)
  blocking collectives  21.3 us (4%)
  between operations  14 us (3%)
  starting transfers between devices  6.01 us (1%)
    all_to_all x1, waiting for transfers between devices, body(): lax.all_to_all(fetched, ('own', 'col'), split_axis=0, concat_axis=0, tile...  152 us
    psum x2, waiting for transfers between devices, extend_area(): local_array = lax.psum(local_array, no)  152 us
    psum x1, waiting for transfers between devices, body(): logits = lax.psum(partial_logits, 'mlp')  42.6 us
    unnamed x20, local copies, waits for them, and re-layouts  38.8 us
    gather x1, local copies, waits for them, and re-layouts, body(): fetched = features[asked_rows]  36.5 us
    all_to_all x1, blocking collectives, body(): lax.all_to_all(requests, ('own', 'col'), split_axis=0, concat_axis=0, til...  21.3 us
    dot_general x1, matrix products, body(): lax.dot_general(received, d_pre, contract_first, preferred_element_type=j...  16.1 us
    scatter x1, local copies, waits for them, and re-layouts, body(): jnp.zeros((owners * capacity,), jnp.int32).at[flat_slot]  15.5 us
  transfers between devices with their start and end apart: 4, of which 4 were waited for; matrix products, arithmetic and copies ran while one was open for 7% of the time, Pallas kernels for 0%

profile of v1, /device:TPU:8, one launch (start us, length us, event | category | flops | bytes accessed | tf_op | source)
XLA Modules:
  0.0 512.9 jit_solution(5483480987417255255)
XLA Ops:
  7.2 0.0 copy-start
  7.2 0.8 add_select_fusion
  8.0 0.1 convert_reduce_fusion
  8.1 0.1 copy.16
  8.2 0.1 reduce_window_sum.23
  8.3 0.1 copy.18
  8.4 0.1 copy.22
  8.5 0.1 reshape.163
  8.6 0.2 reduce_window_sum.22
  8.8 0.1 copy.20
  8.8 0.2 select_reduce_fusion
  9.1 0.1 copy.21
  9.2 0.1 add.89
  9.3 0.1 reshape.145
  9.4 15.5 %scatter_custom_fusion = s32[8192]{0:T(1024)S(1)} fusion(s32[4096]{0:T(1024)S(1)} %bitcast.22, s32[4096]{0:T(1024)S(1)} %reshape.163, s32[]{:T(128)} %constant.41.clone.1), kind=kCustom, calls=%fused_computation.34 | custom fusion | bytes 32772 | tf_op jit(solution)/shard_map/scatter | solution.py:34
  25.0 21.3 %all_to_all.17 = s32[64,1,128]{2,1,0:T(1,128)S(1)} all-to-all(s32[64,1,128]{2,1,0:T(1,128)S(1)} %bitcast.23), channel_id=1, replica_groups=mesh['own'=8,'col'=8,'mlp'=4] {'own','col'}, dimensions={0} | all-to-all | bytes 65536 | tf_op jit(solution)/shard_map/all_to_all | solution.py:36
  46.3 36.5 %gather_fusion = bf16[8192,512]{1,0:T(8,128)(2,1)} fusion(bf16[4096,512]{1,0:T(8,128)(2,1)} %param.6, s32[8192]{0:T(1024)S(1)} %fusion.7), kind=kCustom, calls=%fused_computation | custom fusion | bytes 16809984 | tf_op jit(solution)/shard_map/gather | solution.py:37
  82.8 5.9 %all-to-all-start.1 = ((bf16[64,128,512]{2,1,0:T(8,128)(2,1)}), bf16[64,128,512]{2,1,0:T(8,128)(2,1)}, u32[]{:S(2)}, u32[]{:S(2)}) async-start(bf16[64,128,512]{2,1,0:T(8,128)(2,1)} %bitcast.21), calls=%async_computation.1 | async-start | bytes 16777216 | tf_op jit(solution)/shard_map/all_to_all | solution.py:38
  88.7 0.0 all-reduce.6.cloned.1.call-start
  88.8 0.0 copy-done.4
  88.8 0.1 copy.23
  88.9 0.1 reshape.169
  89.0 0.1 multiply_reduce_fusion
  89.1 0.1 and_reduce_fusion
  89.3 30.4 %scatter_custom_fusion.1 = bf16[1048576]{0:T(1024)(128)(2,1)} fusion(s32[4096]{0:T(1024)S(1)} %broadcast_select_fusion, bf16[4096]{0:T(1024)(128)(2,1)S(1)} %reshape.169, bf16[]{:T(256)} %constant.50.clone.1), kind=kCustom, calls=%fused_computation.10 | custom fusion | bytes 2097154
  119.7 2.8 reshape.150
  122.5 152.3 %all-to-all-done.1 = bf16[64,128,512]{2,1,0:T(8,128)(2,1)} async-done(((bf16[64,128,512]{2,1,0:T(8,128)(2,1)}), bf16[64,128,512]{2,1,0:T(8,128)(2,1)}, u32[]{:S(2)}, u32[]{:S(2)}) %all-to-all-start.1) | async-done | bytes 8388640 | tf_op jit(solution)/shard_map/all_to_all | solution.py:38
  274.8 7.1 %fusion.15 = f32[8192,512]{1,0:T(8,128)S(1)} fusion(bf16[8192,512]{1,0:T(8,128)(2,1)} %bitcast.5, bf16[512,512]{1,0:T(8,128)(2,1)S(1)} %copy-done), kind=kOutput, calls=%fused_computation.43 | convolution fusion | flops 4294967296 | bytes 25690112 | tf_op jit(solution)/shard_map/dot_general | solution.py:49
  281.9 0.0 copy-start.3
  281.9 0.0 copy-start.5
  281.9 1.6 fusion.3
  283.5 4.1 copy-done.1
  287.6 0.8 fusion.16
  288.4 0.0 all-reduce.6.cloned.1.call-update
  288.5 0.0 all-reduce.10.cloned.1.call-start
  288.5 42.6 %all-reduce.6.cloned.1.call-done = f32[128,256]{1,0:T(8,128)} async-done(((f32[128,256]{1,0:T(8,128)}), f32[128,256]{1,0:T(8,128)}) %all-reduce.6.cloned.1.call-update) | async-done | bytes 131088 | tf_op jit(solution)/shard_map/psum | solution.py:53
  331.1 1.0 exponential_reduce_fusion
  332.1 0.0 copy-done.5
  332.1 1.1 convolution_convert_fusion
  333.2 16.1 %fusion.2 = f32[512,512]{1,0:T(8,128)} fusion(bf16[8192,512]{1,0:T(8,128)(2,1)} %bitcast.5, f32[8192,512]{1,0:T(8,128)} %copy-done.1, bf16[128,8192]{1,0:T(8,128)(2,1)S(1)} %reshape.150, bf16[128,512]{1,0:T(8,128)(2,1)S(1)} %convolution_convert_fusion), kind=kOutput, calls=%fused_computation.7 | convolution fusion | flops 5381292032 | bytes 28442624 | tf_op jit(solution)/shard_map/dot_general | solution.py:70
  349.3 1.1 fusion.14
  350.4 0.0 all-reduce.10.cloned.1.call-update
  350.5 0.0 all-reduce.8.cloned.1.call-start
  350.5 80.5 %all-reduce.10.cloned.1.call-done = (f32[512,512]{1,0:T(8,128)}, f32[512,256]{1,0:T(8,128)}) async-done(((f32[512,512]{1,0:T(8,128)}, f32[512,256]{1,0:T(8,128)}), (f32[512,512]{1,0:T(8,128)}, f32[512,256]{1,0:T(8,128)})) %all-reduce.10.cloned.1.call-update) | async-done | bytes 1572880 | tf_op jit(solution)/shard_map/psum | solution.py:9
  431.0 0.0 all-reduce.8.cloned.1.call-update
  431.0 71.2 %all-reduce.8.cloned.1.call-done = (f32[512,512]{1,0:T(8,128)}, f32[512,256]{1,0:T(8,128)}) async-done(((f32[512,512]{1,0:T(8,128)}, f32[512,256]{1,0:T(8,128)}), (f32[512,512]{1,0:T(8,128)}, f32[512,256]{1,0:T(8,128)})) %all-reduce.8.cloned.1.call-update) | async-done | bytes 1572880 | tf_op jit(solution)/shard_map/psum | solution.py:9
  502.2 2.3 copy.29
  504.5 1.9 copy.30
  (17 shorter events, 0.1 us)
Async XLA Ops:
  7.2 267.6 %copy-start = (bf16[512,512]{1,0:T(8,128)(2,1)S(1)}, bf16[512,512]{1,0:T(8,128)(2,1)}, u32[]{:S(2)}) copy-start(bf16[512,512]{1,0:T(8,128)(2,1)} %param.10) | copy-start | bytes 1572868
  82.8 6.0 %copy-start.4 = (bf16[128,32]{0,1:T(8,128)(2,1)S(1)}, bf16[128,32]{0,1:T(8,128)(2,1)}, u32[]{:S(2)}) copy-start(bf16[128,32]{0,1:T(8,128)(2,1)} %param.8) | copy-start | bytes 24580
  82.8 6.2 %copy-start.7 = (s32[2]{0:T(128)S(1)}, s32[2]{0:T(128)}, u32[]{:S(2)}) copy-start(s32[2]{0:T(128)} %constant.51) | copy-start | bytes 28
  82.8 6.3 %copy-start.6 = (s32[2]{0:T(128)S(1)}, s32[2]{0:T(128)}, u32[]{:S(2)}) copy-start(s32[2]{0:T(128)} %constant.54) | copy-start | bytes 28
  82.8 191.9 %all-to-all-start.1 = ((bf16[64,128,512]{2,1,0:T(8,128)(2,1)}), bf16[64,128,512]{2,1,0:T(8,128)(2,1)}, u32[]{:S(2)}, u32[]{:S(2)}) async-start(bf16[64,128,512]{2,1,0:T(8,128)(2,1)} %bitcast.21), calls=%async_computation.1 | async-start | bytes 16777216 | tf_op jit(solution)/shard_map/all_to_all | solution.py:38
  88.7 242.3 %all-reduce.6.cloned.1.call-start = ((), (), s32[]{:S(2)}) async-start(), calls=%async_computation.2 | async-start | bytes 262144 | tf_op jit(solution)/shard_map/psum | solution.py:53
  281.9 5.7 %copy-start.1 = (f32[8192,512]{1,0:T(8,128)}, f32[8192,512]{1,0:T(8,128)S(1)}, u32[]{:S(2)}) copy-start(f32[8192,512]{1,0:T(8,128)S(1)} %fusion.15) | copy-start | bytes 50331652
  281.9 5.7 %copy-start.3 = (bf16[512,256]{1,0:T(8,128)(2,1)S(1)}, bf16[512,256]{1,0:T(8,128)(2,1)}, u32[]{:S(2)}) copy-start(bf16[512,256]{1,0:T(8,128)(2,1)} %param.11) | copy-start | bytes 786436
  281.9 50.2 %copy-start.5 = (s32[128]{0:T(128)S(1)}, s32[128]{0:T(128)}, u32[]{:S(2)}) copy-start(s32[128]{0:T(128)} %param.9) | copy-start | bytes 1540
  288.5 142.5 %all-reduce.10.cloned.1.call-start = ((), (), s32[]{:S(2)}) async-start(), calls=%async_computation.4 | async-start | bytes 3145728 | tf_op jit(solution)/shard_map/psum | solution.py:9
  333.2 16.1 %copy-start.2 = (f32[128,256]{1,0:T(8,128)S(1)}, f32[128,256]{1,0:T(8,128)}, u32[]{:S(2)}) copy-start(f32[128,256]{1,0:T(8,128)} %all-reduce.6.cloned.1.call-done) | copy-start | bytes 393220
  350.5 151.7 %all-reduce.8.cloned.1.call-start = ((), (), s32[]{:S(2)}) async-start(), calls=%async_computation.3 | async-start | bytes 3145728 | tf_op jit(solution)/shard_map/psum | solution.py:9
Sparse Core Ops, SparseCore 0:
  288.6 42.4 all-reduce.5
  350.6 80.3 all-reduce.9
  433.6 68.5 all-reduce.7
